TPU v7x, 512 devices: a whole 4x8x8 slice. The times are simulated.
512 devices in a mesh: views: 4 (over x), depth: 32 (over y, z_hi), lat: 4 (over z_lo, core).
Axes of the slice: x: 4, y: 8, z: 8 (z_hi: 4, z_lo: 2; z = z_hi * 2 + z_lo), core: 2. Of those that a mesh axis runs over, the one named last changes fastest.
Arguments:
- density: bfloat16 [64, 2, 128, 2048], P(None, None, 'depth', 'lat'), may hold values from 0 to 3, as said below
- measured: float32 [16, 64, 2048], P('views', None, 'lat'), may hold values from 0 to 4
- shear_shift: int32 [16, 128], P('views', 'depth'), may hold values from -64 to 63
- shear_frac: float32 [16, 128], P('views', 'depth'), may hold values from 0 to 1
- spectrum: float32 [64], replicated, may hold values from 0.05 to 1
- attenuation: float32 [2, 64], replicated, may hold values from 0.3 to 6
Outputs:
- density_gradient: float32 [64, 2, 128, 2048], P('views', None, 'depth', 'lat')
Inputs may be any that keep to these rules, and one draw needn't show every extreme that they name: `density`: densities are non-negative.
All inputs are finite; a program needn't handle non-finite values.
Results may differ from a plain program's by a relative error of at most 0.0016.
Values may be sent and summed in bfloat16 or wider, within the bound.
A program may use at most 64 MiB of HBM per device.

v0:
```python
import jax
import jax.numpy as jnp
from jax import lax
from jax.sharding import PartitionSpec as P

HALO = 64


def with_halo(x, sides, width):
    for axis, dim in sides:
        size, length = (lax.axis_size(axis), x.shape[dim])
        up = [(i, (i + 1) % size) for i in range(size - 1)]
        down = [(j, i) for i, j in up]
        last = lax.slice_in_dim(x, length - width, length, axis=dim)
        first = lax.slice_in_dim(x, 0, width, axis=dim)
        before = lax.ppermute(last, axis, up)
        after = lax.ppermute(first, axis, down)
        x = jnp.concatenate([before, x, after], axis=dim)
    return x


def band_forward(shear_shift, lower_weight, upper_weight, window, block_width):
    band_shape = (shear_shift.shape[1], window, shear_shift.shape[0], block_width)
    tap_index = lax.broadcasted_iota(jnp.int32, band_shape, 1)
    column = lax.broadcasted_iota(jnp.int32, band_shape, 3)
    anchor = (shear_shift.T + HALO)[:, None, :, None]
    nothing = jnp.zeros((), jnp.bfloat16)
    lower_part = jnp.where(tap_index == column + anchor, lower_weight.T[:, None, :, None], nothing)
    upper_part = jnp.where(
        tap_index == column + anchor + 1, upper_weight.T[:, None, :, None], nothing
    )
    return lower_part + upper_part


def band_backward(shear_shift, lower_weight, upper_weight, window, block_width):
    band_shape = (shear_shift.shape[0], window, shear_shift.shape[1], block_width)
    tap_index = lax.broadcasted_iota(jnp.int32, band_shape, 1)
    column = lax.broadcasted_iota(jnp.int32, band_shape, 3)
    anchor = (HALO - shear_shift)[:, None, :, None]
    nothing = jnp.zeros((), jnp.bfloat16)
    lower_part = jnp.where(tap_index == column + anchor, lower_weight[:, None, :, None], nothing)
    upper_part = jnp.where(
        tap_index == column + anchor - 1, upper_weight[:, None, :, None], nothing
    )
    return lower_part + upper_part


def spectral(path_sums, observed, spectrum, attenuation, views_all):
    view_count, row_count, materials, tile_width = path_sums.shape
    block_pixels = 4096
    path_water = path_sums[:, :, 0, :].reshape(-1, block_pixels)
    path_bone = path_sums[:, :, 1, :].reshape(-1, block_pixels)
    target_flat = observed.reshape(-1, block_pixels)
    coefficients = jnp.concatenate(
        [jnp.ones((1, spectrum.shape[0]), jnp.float32), attenuation], axis=0
    )
    emitted = jnp.log(jnp.sum(spectrum))

    def one_block(inputs):
        water_block, bone_block, target_block = inputs
        exponent = (
            attenuation[0][:, None] * water_block[None, :]
            + attenuation[1][:, None] * bone_block[None, :]
        )
        counts = spectrum[:, None] * jnp.exp(-exponent)
        moments = jnp.dot(coefficients, counts, precision=lax.Precision.HIGHEST)
        intensity = moments[0]
        residual = emitted - jnp.log(intensity) - target_block
        factor = residual / intensity / views_all
        return (moments[1:] * factor[None, :]).astype(jnp.bfloat16)

    stacked = lax.map(one_block, (path_water, path_bone, target_flat))
    gradients = jnp.swapaxes(stacked, 0, 1).reshape(materials, view_count, row_count, tile_width)
    return jnp.transpose(gradients, (1, 2, 0, 3))


def per_device(density, measured, shear_shift, shear_frac, spectrum, attenuation):
    row_total, materials, depth_here, tile_width = density.shape
    block_width = min(128, tile_width)
    block_count = tile_width // block_width
    window = block_width + 2 * HALO
    views_all = measured.shape[0] * lax.axis_size("views")
    depth_all = depth_here * lax.axis_size("depth")
    rows_out = row_total // lax.axis_size("views")
    lower_weight = (1.0 - shear_frac).astype(jnp.bfloat16)
    upper_weight = shear_frac.astype(jnp.bfloat16)
    rows_here = density.shape[0]
    padded = with_halo(density, (("lat", 3),), HALO)
    framed = jnp.stack(
        [
            padded[:, :, :, number * block_width : number * block_width + window]
            for number in range(block_count)
        ],
        axis=2,
    )
    forward_band = band_forward(shear_shift, lower_weight, upper_weight, window, block_width)
    partial_value = jnp.einsum(
        "ymnzi,zivc->vymnc", framed, forward_band, preferred_element_type=jnp.float32
    )
    partial_value = partial_value.reshape(shear_shift.shape[0], rows_here, materials, tile_width)
    path_sums = lax.psum(partial_value, "depth") / depth_all
    path_grads = spectral(path_sums, measured, spectrum, attenuation, views_all)
    padded_grads = with_halo(path_grads, (("lat", 3),), HALO)
    framed_grads = jnp.stack(
        [
            padded_grads[:, :, :, number * block_width : number * block_width + window]
            for number in range(block_count)
        ],
        axis=3,
    )
    backward_band = band_backward(shear_shift, lower_weight, upper_weight, window, block_width)
    product = jnp.einsum(
        "vymni,vizc->ymznc", framed_grads, backward_band, preferred_element_type=jnp.float32
    )
    return lax.psum_scatter(
        product.reshape(rows_out * lax.axis_size("views"), materials, depth_here, tile_width),
        "views",
        scatter_dimension=0,
        tiled=True,
    )


def solution(mesh):
    in_specs = (
        P(None, None, "depth", "lat"),
        P("views", None, "lat"),
        P("views", "depth"),
        P("views", "depth"),
        P(),
        P(),
    )
    out_specs = P("views", None, "depth", "lat")
    return jax.shard_map(
        per_device, mesh=mesh, in_specs=in_specs, out_specs=out_specs, check_vma=False
    )
```

profile of v0, /device:TPU:8, one launch (start us, length us, event | category | flops | bytes accessed | tf_op | source)
XLA Modules:
  0.0 428.9 jit_solution(15175280310267215764)
XLA Ops:
  6.5 1.2 copy.23
  7.9 1.7 collective-permute-start
  9.6 1.3 collective-permute-start.1
  11.0 4.0 collective-permute-done.1
  15.6 1.1 convolution_bitcast_fusion.2
  16.7 1.1 copy.42
  18.0 1.0 copy-done
  20.3 321.3 %all-reduce.3.cloned.1.call-done = f32[4,64,2,512]{3,1,2,0:T(8,128)} async-done(((f32[4,64,2,512]{3,1,2,0:T(8,128)}), f32[4,64,2,512]{3,1,2,0:T(8,128)}) %all-reduce.3.cloned.1.call-update) | async-done | bytes 1048592 | tf_op jit(solution)/shard_map/psum | solution.py:101
  341.6 1.4 broadcast_multiply_fusion
  343.3 35.3 %while.10 = (s32[]{:T(128)}, bf16[32,2,4096]{2,1,0:T(2,128)(2,1)S(1)}, f32[64]{0:T(128)S(1)}, f32[2,64]{1,0:T(2,128)S(1)}, f32[32,4096]{1,0:T(8,128)S(1)}, /*ind...) while((s32[]{:T(128)}, ...), condition=%wide.region_3.4_spmd, body=%wide.region_2.3_spmd.sunk | while | flops 10780674 | bytes 264821 | solution.py:72
  344.4 0.9 convolution_bitcast_fusion.4
  345.5 0.9 convolution_bitcast_fusion.4
  346.7 0.9 convolution_bitcast_fusion.4
  347.8 0.9 convolution_bitcast_fusion.4
  348.9 0.9 convolution_bitcast_fusion.4
  350.0 0.9 convolution_bitcast_fusion.4
  351.1 0.9 convolution_bitcast_fusion.4
  352.2 0.9 convolution_bitcast_fusion.4
  353.3 0.9 convolution_bitcast_fusion.4
  354.4 0.9 convolution_bitcast_fusion.4
  355.5 0.9 convolution_bitcast_fusion.4
  357.7 0.9 convolution_bitcast_fusion.4
  358.8 0.9 convolution_bitcast_fusion.4
  359.9 0.9 convolution_bitcast_fusion.4
  361.0 0.9 convolution_bitcast_fusion.4
  379.2 1.3 collective-permute-start.2
  380.5 1.3 collective-permute-start.3
  382.1 3.1 collective-permute-done.3
  385.8 1.1 convolution_bitcast_fusion.1
  387.6 1.4 reshape.24
  389.0 31.2 %reduce-scatter.2.cloned.1.call-done = f32[16,2,4,512]{3,0,2,1:T(8,128)} async-done(((f32[64,2,4,512]{3,0,2,1:T(8,128)}), f32[16,2,4,512]{3,0,2,1:T(8,128)}) %reduce-scatter.2.cloned.1.call-update) | async-done | bytes 262160 | tf_op jit(solution)/shard_map/reduce_scatter | solution.py:115
  420.3 1.8 copy.35
  (179 shorter events, 24.1 us)
Async XLA Ops:
  6.5 4.4 %copy-start.2 = (s32[4,4]{1,0:T(4,128)S(1)}, s32[4,4]{1,0:T(4,128)}, u32[]{:S(2)}) copy-start(s32[4,4]{1,0:T(4,128)} %param.10) | copy-start | bytes 196
  6.5 4.4 %copy-start.3 = (f32[4,4]{1,0:T(4,128)S(1)}, f32[4,4]{1,0:T(4,128)}, u32[]{:S(2)}) copy-start(f32[4,4]{1,0:T(4,128)} %param.11) | copy-start | bytes 196
  6.5 335.1 %all-reduce.3.cloned.1.call-start = ((), (), s32[]{:S(2)}) async-start(), calls=%async_computation.1 | async-start | bytes 2097152 | tf_op jit(solution)/shard_map/psum | solution.py:101
  7.9 3.1 collective-permute-start
  9.6 5.4 %collective-permute-start.1 = (bf16[64,2,4,64]{3,0,2,1:T(8,128)(2,1)S(1)}, bf16[64,2,4,64]{3,0,2,1:T(8,128)(2,1)S(1)}, u32[]{:S(2)}, u32[]{:S(2)}) collective-permute-start(bf16[64,2,4,64]{3,0,2,1:T(8,128)(2,1)S(1)} %get-tuple-element.88), channel_id=1, source_target_pairs={{1,0},{2,1},{3,2},{5,4},{6,5},{7,6},{9,8},{10,9},{11,10},{13,12},{... | collective-permute-start | bytes 196616 | tf_op jit(solution)/shard_map/ppermute | solution.py:17
  17.9 1.0 copy-start
  17.9 1.1 copy-start.4
  17.9 2.4 copy-start.1
  17.9 402.4 %reduce-scatter.2.cloned.1.call-start = ((), (), s32[]{:S(2)}) async-start(), calls=%async_computation.2 | async-start | bytes 1310720 | tf_op jit(solution)/shard_map/reduce_scatter | solution.py:115
  379.2 2.9 collective-permute-start.2
  380.5 4.7 %collective-permute-start.3 = (bf16[4,64,2,64]{3,1,0,2:T(8,128)(2,1)S(1)}, bf16[4,64,2,64]{3,1,0,2:T(8,128)(2,1)S(1)}, u32[]{:S(2)}, u32[]{:S(2)}) collective-permute-start(bf16[4,64,2,64]{3,1,0,2:T(8,128)(2,1)S(1)} %get-tuple-element.82), channel_id=1, source_target_pairs={{1,0},{2,1},{3,2},{5,4},{6,5},{7,6},{9,8},{10,9},{11,10},{13,12},{... | collective-permute-start | bytes 196616 | tf_op jit(solution)/shard_map/ppermute | solution.py:17
Sparse Core Ops, SparseCore 0:
  18.0 323.5 all-reduce.2
  389.1 31.0 reduce-scatter.1
where the time goes:
time: 429 us
  waiting for transfers between devices  360 us (84%)
  matrix products  31.8 us (7%)
  between operations  14.3 us (3%)
  local copies, waits for them, and re-layouts  9.82 us (2%)
  other arithmetic  6.36 us (1%)
  starting transfers between devices  5.67 us (1%)
    psum x1, waiting for transfers between devices, per_device(): path_sums = lax.psum(partial_value, 'depth') / depth_all  321 us
    reduce_scatter x1, waiting for transfers between devices, per_device(): lax.psum_scatter(product.reshape(rows_out * lax.axis_size('views'), mater...  31.2 us
    dot_general x32, matrix products, one_block(): moments = jnp.dot(coefficients, counts, precision=lax.Precision.HIGHEST)  29.5 us
  transfers between devices with their start and end apart: 6, of which 4 were waited for; matrix products, arithmetic and copies ran while one was open for 0% of the time, Pallas kernels for 0%

commit v1 on v0

--- a/solution.py
+++ b/solution.py
@@ -2,6 +2,7 @@
 import jax.numpy as jnp
 from jax import lax
 from jax.sharding import PartitionSpec as P
+from jax.lax import all_gather
 
 HALO = 64
 
@@ -75,6 +76,10 @@
 
 
 def per_device(density, measured, shear_shift, shear_frac, spectrum, attenuation):
+
+    def _expand_fields(frame):
+        return all_gather(frame, axis_name="depth").sum(axis=0)
+
     row_total, materials, depth_here, tile_width = density.shape
     block_width = min(128, tile_width)
     block_count = tile_width // block_width
@@ -98,7 +103,7 @@
         "ymnzi,zivc->vymnc", framed, forward_band, preferred_element_type=jnp.float32
     )
     partial_value = partial_value.reshape(shear_shift.shape[0], rows_here, materials, tile_width)
-    path_sums = lax.psum(partial_value, "depth") / depth_all
+    path_sums = _expand_fields(partial_value) / depth_all
     path_grads = spectral(path_sums, measured, spectrum, attenuation, views_all)
     padded_grads = with_halo(path_grads, (("lat", 3),), HALO)
     framed_grads = jnp.stack(

time: 429 us -> 508 us (1.18)
  waiting for transfers between devices: 360 us -> 426 us
  other arithmetic: 6.36 us -> 18.8 us
    all_gather x0 -> x1, waiting for transfers between devices: none -> 391 us  [_expand_fields(): return all_gather(frame, axis_name='depth').sum(axis=0)]
    psum x1 -> x0, waiting for transfers between devices: 321 us -> none  [per_device(): path_sums = lax.psum(partial_value, 'depth') / depth_all]
    reduce_sum x0 -> x1, other arithmetic: none -> 12.3 us  [_expand_fields(): return all_gather(frame, axis_name='depth').sum(axis=0)]
where the time goes in v1:
time: 508 us
  waiting for transfers between devices  426 us (84%)
  matrix products  31.8 us (6%)
  other arithmetic  18.8 us (4%)
  between operations  14.3 us (3%)
  local copies, waits for them, and re-layouts  9.83 us (2%)
  starting transfers between devices  5.72 us (1%)
    all_gather x1, waiting for transfers between devices, _expand_fields(): return all_gather(frame, axis_name='depth').sum(axis=0)  391 us
    reduce_scatter x1, waiting for transfers between devices, per_device(): lax.psum_scatter(product.reshape(rows_out * lax.axis_size('views'), mater...  30.9 us
    dot_general x32, matrix products, one_block(): moments = jnp.dot(coefficients, counts, precision=lax.Precision.HIGHEST)  29.5 us
    reduce_sum x1, other arithmetic, _expand_fields(): return all_gather(frame, axis_name='depth').sum(axis=0)  12.3 us
  transfers between devices with their start and end apart: 6, of which 4 were waited for; matrix products, arithmetic and copies ran while one was open for 0% of the time, Pallas kernels for 0%

profile of v1, /device:TPU:8, one launch (start us, length us, event | category | flops | bytes accessed | tf_op | source)
XLA Modules:
  0.0 507.9 jit_solution(1377331811171550004)
XLA Ops:
  6.5 1.2 copy.39
  7.8 1.7 collective-permute-start
  9.6 1.3 collective-permute-start.1
  12.4 2.6 collective-permute-done.1
  15.6 1.1 convolution_bitcast_fusion.2
  17.4 1.4 all_gather_reshape.3
  20.4 390.8 %all-gather.2.cloned.1.call-done = f32[32,4,64,2,512]{4,2,3,1,0:T(8,128)} async-done(((f32[1,4,64,2,512]{4,2,3,1,0:T(8,128)}), f32[32,4,64,2,512]{4,2,3,1,0:T(8,128)}) %all-gather.2.cloned.1.call-update) | async-done | bytes 33554448 | tf_op jit(solution)/shard_map/all_gather | solution.py:81
  411.2 12.3 %reduce_sum.18 = f32[4,64,2,512]{3,1,2,0:T(8,128)S(1)} reduce(f32[32,4,64,2,512]{4,2,3,1,0:T(8,128)} %all-gather.2.cloned.1.call-done, f32[]{:T(128)} %constant.31.clone.1), dimensions={0}, to_apply=%region_0.1 | reduce | flops 8126464 | bytes 34603012 | tf_op jit(solution)/shard_map/reduce_sum | solution.py:81
  424.0 35.3 %while.10 = (s32[]{:T(128)}, bf16[32,2,4096]{2,1,0:T(2,128)(2,1)S(1)}, f32[64]{0:T(128)S(1)}, f32[2,64]{1,0:T(2,128)S(1)}, f32[32,4096]{1,0:T(8,128)S(1)}, /*ind...) while((s32[]{:T(128)}, ...), condition=%wide.region_3.4_spmd, body=%wide.region_2.3_spmd.sunk | while | flops 10780674 | bytes 264821 | solution.py:73
  425.1 0.9 convolution_bitcast_fusion.4
  426.2 0.9 convolution_bitcast_fusion.4
  427.3 0.9 convolution_bitcast_fusion.4
  428.4 0.9 convolution_bitcast_fusion.4
  429.5 0.9 convolution_bitcast_fusion.4
  430.6 0.9 convolution_bitcast_fusion.4
  431.7 0.9 convolution_bitcast_fusion.4
  432.8 0.9 convolution_bitcast_fusion.4
  433.9 0.9 convolution_bitcast_fusion.4
  435.0 0.9 convolution_bitcast_fusion.4
  436.1 0.9 convolution_bitcast_fusion.4
  438.3 0.9 convolution_bitcast_fusion.4
  439.5 0.9 convolution_bitcast_fusion.4
  440.6 0.9 convolution_bitcast_fusion.4
  441.7 0.9 convolution_bitcast_fusion.4
  442.8 0.9 convolution_bitcast_fusion.4
  459.9 1.3 collective-permute-start.2
  461.3 1.3 collective-permute-start.3
  462.9 1.6 collective-permute-done.3
  465.1 1.1 convolution_bitcast_fusion.1
  466.9 1.4 reshape.20
  468.3 30.9 %reduce-scatter.2.cloned.1.call-done = f32[16,2,4,512]{3,0,2,1:T(8,128)} async-done(((f32[64,2,4,512]{3,0,2,1:T(8,128)}), f32[16,2,4,512]{3,0,2,1:T(8,128)}) %reduce-scatter.2.cloned.1.call-update) | async-done | bytes 262160 | tf_op jit(solution)/shard_map/reduce_scatter | solution.py:120
  499.2 1.8 copy.51
  (177 shorter events, 25.4 us)
Async XLA Ops:
  6.5 404.7 %all-gather.2.cloned.1.call-start = ((), (), s32[]{:S(2)}) async-start(), calls=%async_computation.1 | async-start | bytes 34603008 | tf_op jit(solution)/shard_map/all_gather | solution.py:81
  7.8 4.5 collective-permute-start
  9.6 5.4 %collective-permute-start.1 = (bf16[64,2,4,64]{3,0,2,1:T(8,128)(2,1)S(1)}, bf16[64,2,4,64]{3,0,2,1:T(8,128)(2,1)S(1)}, u32[]{:S(2)}, u32[]{:S(2)}) collective-permute-start(bf16[64,2,4,64]{3,0,2,1:T(8,128)(2,1)S(1)} %get-tuple-element.88), channel_id=1, source_target_pairs={{1,0},{2,1},{3,2},{5,4},{6,5},{7,6},{9,8},{10,9},{11,10},{13,12},{... | collective-permute-start | bytes 196616 | tf_op jit(solution)/shard_map/ppermute | solution.py:18
  17.4 1.5 copy-start
  17.4 1.6 copy-start.2
  17.4 2.9 copy-start.1
  18.9 480.3 %reduce-scatter.2.cloned.1.call-start = ((), (), s32[]{:S(2)}) async-start(), calls=%async_computation.2 | async-start | bytes 1310720 | tf_op jit(solution)/shard_map/reduce_scatter | solution.py:120
  459.9 3.0 collective-permute-start.2
  461.3 3.2 collective-permute-start.3
Sparse Core Ops, SparseCore 0:
  19.0 392.1 all-gather.1
  468.4 30.7 reduce-scatter.1
